TPU v7x, 32 devices: a whole 2x2x4 slice. The times are simulated.
32 devices in a mesh: ka: 8 (over z, y), band: 2 (over x), ga: 2 (over core).
Axes of the slice: x: 2, y: 2, z: 4, core: 2. Of those that a mesh axis runs over, the one named last changes fastest.
Arguments:
- pair_density: bfloat16 [8, 256, 8, 2048], P(None, ('ka', 'band')), may hold values from -4 to 4
- valence_energy: float32 [8, 8], replicated, may hold values from -6 to -1
- conduction_energy: float32 [8, 256], replicated, may hold values from 0.5 to 12
- star_map: int32 [64], replicated, may hold values from 0 to 7, as said below
- op_of_k: int32 [64], replicated, may hold values from 0 to 47
- perm_lists: int32 [48, 2048], replicated, may hold values from 0 to 2047, as said below
- cond_top: int32 [64], replicated, may hold values from 128 to 256
Outputs:
- chi: float32 [1, 2048, 2048], P(None, ('band', 'ga'), 'ka')
Inputs may be any that keep to these rules, and one draw needn't show every extreme that they name: `star_map`: every irreducible point is named by at least one full-zone k-point. `perm_lists`: each row is a permutation of 0 .. 2047 that maps every aligned block of 128 slots onto itself.
All inputs are finite; a program needn't handle non-finite values.
Results may differ from a plain program's by a relative error of at most 0.0015.
Values may be sent and summed in bfloat16 or wider, within the bound.
A program may use at most 320 MiB of HBM per device.

v0:
```python
import jax
import jax.numpy as jnp
from jax import lax
from jax.sharding import PartitionSpec as P

NG = 2048
GB = 128
KI = 8
KF = 64
NF = 1


freq_step = 2.0


def rotate_batch(picked, perm_rows):
    k_count = picked.shape[0]
    blocks = NG // GB
    local = perm_rows.reshape(k_count, blocks, GB) - (jnp.arange(blocks) * GB)[None, :, None]
    onehot = (local[..., None] == jnp.arange(GB)[None, None, None, :]).astype(jnp.bfloat16)
    shaped = picked.reshape(k_count, -1, blocks, GB)
    moved = jnp.einsum("krbi,kboi->krbo", shaped, onehot, preferred_element_type=jnp.float32)
    return moved.astype(jnp.bfloat16).reshape(picked.shape)


def on_device(
    pair_density, valence_energy, conduction_energy, star_map, op_of_k, perm_lists, cond_top
):
    ka_count = lax.axis_size("ka")
    band_count = lax.axis_size("band")
    ga_count = lax.axis_size("ga")
    ka_index = lax.axis_index("ka")
    band_index = lax.axis_index("band")
    ga_index = lax.axis_index("ga")
    k_local = KF // ka_count
    cond_piece = pair_density.shape[1]
    my_points = ka_index * k_local + jnp.arange(k_local)
    stars = jnp.take(star_map, my_points)
    tops = jnp.take(cond_top, my_points)
    whole = lax.all_gather(pair_density, "ka", axis=1, tiled=True)
    picked = jnp.take(whole, stars, axis=0)
    my_perms = jnp.take(perm_lists, jnp.take(op_of_k, my_points), axis=0)
    rotated = rotate_batch(picked, my_perms)
    cond_table = conduction_energy.reshape(KI, ka_count, band_count, cond_piece)
    cond_table = lax.dynamic_slice_in_dim(cond_table, band_index, 1, 2).reshape(
        KI, ka_count * cond_piece
    )
    cond_local = jnp.take(cond_table, stars, axis=0)
    val_local = jnp.take(valence_energy, stars, axis=0)
    band_global = (
        jnp.arange(ka_count)[:, None] * band_count + band_index
    ) * cond_piece + jnp.arange(cond_piece)[None, :]
    band_global = band_global.reshape(ka_count * cond_piece)
    mask = (band_global[None, :] < tops[:, None]).astype(jnp.float32)[None, :, :, None]
    omega = freq_step * jnp.arange(NF).astype(jnp.float32)
    omega_sq = (omega * omega)[:, None, None, None]
    diff = val_local[:, None, :] - cond_local[:, :, None]
    weight = 4.0 / KF * diff[None] / (diff[None] * diff[None] + omega_sq) * mask
    product = weight[..., None] * rotated[None].astype(jnp.float32)
    scaled_hi = product.astype(jnp.bfloat16)
    hi_back = lax.optimization_barrier(scaled_hi).astype(jnp.float32)
    scaled_lo = (product - hi_back).astype(jnp.bfloat16)
    pair_rows = rotated.shape[0] * rotated.shape[1] * rotated.shape[2]
    flat_scaled = jnp.stack(
        [scaled_hi.reshape(NF, pair_rows, NG), scaled_lo.reshape(NF, pair_rows, NG)]
    )
    flat = rotated.reshape(pair_rows, NG)
    slab = NG // (band_count * ga_count)
    row_part = flat.reshape(pair_rows, band_count, ga_count, slab)
    row_part = lax.dynamic_slice_in_dim(row_part, ga_index, 1, 2).reshape(
        pair_rows, band_count * slab
    )
    partial_value = jnp.einsum(
        "rg,sfrh->fgh", row_part, flat_scaled, preferred_element_type=jnp.float32
    )
    column_sums = lax.psum_scatter(partial_value, "ka", scatter_dimension=2, tiled=True)
    return lax.psum_scatter(column_sums, "band", scatter_dimension=1, tiled=True)


def solution(mesh):
    return jax.shard_map(
        on_device,
        mesh=mesh,
        in_specs=(P(None, ("ka", "band"), None, None), P(), P(), P(), P(), P(), P()),
        out_specs=P(None, ("band", "ga"), "ka"),
        check_vma=False,
    )
```

profile of v0, /device:TPU:0, one launch (start us, length us, event | category | flops | bytes accessed | tf_op | source)
XLA Modules:
  0.0 1458.4 jit_solution(7433224943358590630)
XLA Ops:
  6.5 0.0 copy-start
  6.5 0.0 all-gather.2.cloned.1.call-start
  6.5 0.7 all-gather.2.cloned.1.call-update
  7.3 0.0 reduce-scatter.3.cloned.1.call-start
  7.3 1.3 gather_fusion.8
  8.6 1.3 gather_fusion.7
  9.9 1.3 gather_fusion.6
  11.3 0.1 iota_add_fusion
  11.3 0.1 add.71
  11.4 0.0 copy-done
  11.5 0.6 gather_fusion.2
  12.0 0.1 fusion.7
  12.2 0.8 reshape.251
  13.0 0.1 reshape.252
  13.1 1.2 gather_fusion
  14.4 0.6 gather_fusion.1
  14.9 0.1 compare_convert_fusion
  15.0 0.1 broadcast_select_fusion.1
  15.1 0.1 broadcast_select_fusion
  15.2 0.3 fusion.6
  15.5 0.0 copy-start.2
  15.5 0.8 mul.115
  16.4 633.0 %all-gather.2.cloned.1.call-done = bf16[8,128,8,2048]{3,2,1,0:T(8,128)(2,1)} async-done(((bf16[8,16,8,2048]{3,2,1,0:T(8,128)(2,1)}), bf16[8,128,8,2048]{3,2,1,0:T(8,128)(2,1)}) %all-gather.2.cloned.1.call-update) | async-done | bytes 33554448 | tf_op jit(solution)/shard_map/all_gather | solution.py:40
  649.4 17.1 %fusion.9 = (bf16[8,128,8,768]{3,2,1,0:T(8,128)(2,1)}, bf16[8,128,8,768]{3,2,1,0:T(8,128)(2,1)}) fusion(bf16[8,128,8,2048]{3,2,1,0:T(8,128)(2,1)} %all-gather.2.cloned.1.call-done), kind=kLoop, calls=%fused_computation.48 | loop fusion | bytes 50331648 | tf_op jit(solution)/shard_map/jit(_take)/gather | solution.py:41
  666.5 10.9 gather_fusion.3
  677.4 0.0 copy-done.2
  677.4 7.1 mini-gather-slice.5
  684.5 8.1 gather_fusion.5
  692.6 10.9 gather_fusion.4
  703.5 23.0 %pad_maximum_fusion = bf16[8,128,8,2048]{3,2,1,0:T(8,128)(2,1)} fusion(bf16[8,128,8,512]{3,2,1,0:T(8,128)(2,1)} %gather_fusion.5, bf16[8,128,8,768]{3,2,1,0:T(8,128)(2,1)} %gather_fusion.4, bf16[8,128,8,768]{3,2,1,0:T(8,128)(2,1)} %gather_fusion.3), kind=kLoop, calls=%fused_computation.14 | loop fusion | flops 100663296 | bytes 67108864
  726.5 23.1 %copy.20 = bf16[1024,8,16,128]{3,2,1,0:T(8,128)(2,1)} copy(bf16[1024,8,16,128]{3,1,2,0:T(8,128)(2,1)} %bitcast.37) | data formatting | bytes 67108864
  749.6 56.6 %convert_bitcast_fusion = bf16[8,1024,16,128]{1,3,2,0:T(8,128)(2,1)} fusion(bf16[8,1024,16,128]{3,2,1,0:T(8,128)(2,1)} %bitcast.38, pred[8]{0:T(512)(128)(4,1)S(1)} %get-tuple-element.12, s32[8,16,128]{2,1,0:T(8,128)S(1)} %copy.13), kind=kOutput, calls=%fused_computation.17 | convolution fusion | flops 4330618880 | bytes 67174408 | tf_op jit(solution)/shard_map/krbi,kboi->krbo/dot_general | solution.py:22
  806.2 30.9 %copy.17 = bf16[8,1024,16,128]{1,0,3,2:T(8,128)(2,1)} copy(bf16[8,1024,16,128]{1,3,2,0:T(8,128)(2,1)} %convert_bitcast_fusion) | data formatting | bytes 67108864 | tf_op jit(solution)/shard_map/convert_element_type | solution.py:23
  837.1 49.6 %copy.15 = f32[8,1024,16,128]{3,2,1,0:T(8,128)} copy(bf16[8,1024,16,128]{1,3,2,0:T(8,128)(2,1)} %convert_bitcast_fusion) | data formatting | bytes 100663296 | tf_op jit(solution)/shard_map/convert_element_type | solution.py:59
  886.7 70.4 %reshape.255 = f32[1,8,128,8,2048]{4,3,2,1,0:T(8,128)} reshape(f32[8,1024,16,128]{3,2,1,0:T(8,128)} %copy.15) | data formatting | bytes 134217728 | tf_op jit(solution)/shard_map/convert_element_type | solution.py:59
  957.1 70.4 %reshape.254 = f32[1,8192,2048]{2,1,0:T(8,128)} reshape(f32[8,1024,16,128]{3,2,1,0:T(8,128)} %copy.15) | data formatting | bytes 134217728 | tf_op jit(solution)/shard_map/convert_element_type | solution.py:59
  1027.5 0.0 copy-start.3
  1027.5 50.0 %reshape_reshape_reshape.3 = bf16[8192,2,2,512]{0,3,2,1:T(8,128)(2,1)} reshape(bf16[8,1024,16,128]{1,0,3,2:T(8,128)(2,1)} %copy.17) | data formatting | bytes 67108864 | tf_op jit(solution)/shard_map/reshape;reshape;reshape | solution.py:69
  1077.5 0.0 copy-done.3
  1077.5 32.4 %multiply_convert_fusion.1 = bf16[1,8,128,8,2048]{4,3,2,1,0:T(8,128)(2,1)} fusion(f32[1,8,128,8,2048]{4,3,2,1,0:T(8,128)} %reshape.255, f32[8,128,8]{2,1,0:T(8,128)S(1)} %copy-done.3), kind=kLoop, calls=%fused_computation.12 | loop fusion | flops 33554432 | bytes 100696064 | tf_op jit(solution)/shard_map/convert_element_type | solution.py:60
  1109.9 42.4 %subtract_convert_fusion = bf16[1,8,128,8,2048]{4,3,2,1,0:T(8,128)(2,1)} fusion(bf16[1,8,128,8,2048]{4,3,2,1,0:T(8,128)(2,1)} %multiply_convert_fusion.1, f32[1,8,128,8,2048]{4,3,2,1,0:T(8,128)} %reshape.255, f32[8,128,8]{2,1,0:T(8,128)S(1)} %copy-done.3), kind=kLoop, calls=%fused_computation.10 | loop fusion | flops 67108864 | bytes 134250496 | tf_op jit(solution)/shard_map/convert_element_type | solution.py:62
  1152.2 0.0 copy-start.4
  1152.2 13.9 constant_dynamic-slice_fusion
  1166.1 0.0 copy-done.4
  1166.1 32.5 %fusion = bf16[1,1,8192,2048]{3,2,1,0:T(8,128)(2,1)} fusion(f32[1,8192,2048]{2,1,0:T(8,128)} %reshape.254, f32[8192]{0:T(1024)S(1)} %copy-done.4), kind=kLoop, calls=%fused_computation.13 | loop fusion | flops 33554432 | bytes 100696064 | tf_op jit(solution)/shard_map/stack | solution.py:64
  1198.6 36.7 %convert_reduce_fusion = bf16[8192,2048]{1,0:T(8,128)(2,1)} fusion(bf16[1,1,8192,2048]{3,2,1,0:T(8,128)(2,1)} %bitcast.36, bf16[1,1,8192,2048]{3,2,1,0:T(8,128)(2,1)} %fusion), kind=kLoop, calls=%fused_computation.9 | loop fusion | flops 150994944 | bytes 100663296 | tf_op jit(solution)/shard_map/rg,sfrh->fgh/reduce_sum | solution.py:73
  1235.2 0.0 copy-start.1
  1235.3 43.7 %convolution_bitcast_fusion = f32[1,1024,2048]{1,2,0:T(8,128)} fusion(bf16[8192,2048]{1,0:T(8,128)(2,1)} %convert_reduce_fusion, bf16[8192,1024]{0,1:T(8,128)(2,1)} %bitcast.39), kind=kOutput, calls=%fused_computation.21 | convolution fusion | flops 34359738368 | bytes 58720256 | tf_op jit(solution)/shard_map/rg,sfrh->fgh/dot_general | solution.py:73
  1279.0 0.0 reduce-scatter.3.cloned.1.call-update
  1279.0 0.0 reduce-scatter.5.cloned.1.call-start
  1279.1 149.1 %reduce-scatter.3.cloned.1.call-done = f32[1,1024,256]{1,2,0:T(8,128)} async-done(((f32[1,1024,2048]{1,2,0:T(8,128)}), f32[1,1024,256]{1,2,0:T(8,128)}) %reduce-scatter.3.cloned.1.call-update) | async-done | bytes 1048592 | tf_op jit(solution)/shard_map/reduce_scatter | solution.py:76
  1428.2 0.0 reduce-scatter.5.cloned.1.call-update
  1428.2 21.6 %reduce-scatter.5.cloned.1.call-done = f32[1,512,256]{1,2,0:T(8,128)} async-done(((f32[1,1024,256]{1,2,0:T(8,128)}), f32[1,512,256]{1,2,0:T(8,128)}) %reduce-scatter.5.cloned.1.call-update) | async-done | bytes 524304 | tf_op jit(solution)/shard_map/reduce_scatter | solution.py:77
  1449.8 2.0 copy.18
  1451.9 0.0 copy-done.1
  (10 shorter events, 0.1 us)
Async XLA Ops:
  6.5 4.9 copy-start
  6.5 642.8 %all-gather.2.cloned.1.call-start = ((), (), s32[]{:S(2)}) async-start(), calls=%async_computation.2 | async-start | bytes 37748736 | tf_op jit(solution)/shard_map/all_gather | solution.py:40
  7.3 1420.9 %reduce-scatter.3.cloned.1.call-start = ((), (), s32[]{:S(2)}) async-start(), calls=%async_computation.3 | async-start | bytes 9437184 | tf_op jit(solution)/shard_map/reduce_scatter | solution.py:76
  15.5 661.9 %copy-start.2 = (f32[8,128,8]{2,1,0:T(8,128)}, f32[8,128,8]{2,1,0:T(8,128)S(1)}, u32[]{:S(2)}) copy-start(f32[8,128,8]{2,1,0:T(8,128)S(1)} %fusion.6) | copy-start | bytes 98308
  1027.5 50.0 %copy-start.3 = (f32[8,128,8]{2,1,0:T(8,128)S(1)}, f32[8,128,8]{2,1,0:T(8,128)}, u32[]{:S(2)}) copy-start(f32[8,128,8]{2,1,0:T(8,128)} %copy-done.2) | copy-start | bytes 98308
  1152.2 13.9 copy-start.4
  1235.2 216.6 %copy-start.1 = (s32[48,2048]{1,0:T(8,128)S(1)}, s32[48,2048]{1,0:T(8,128)}, u32[]{:S(2)}) copy-start(s32[48,2048]{1,0:T(8,128)} %param.14) | copy-start | bytes 1179652
  1279.0 170.8 %reduce-scatter.5.cloned.1.call-start = ((), (), s32[]{:S(2)}) async-start(), calls=%async_computation.4 | async-start | bytes 1572864 | tf_op jit(solution)/shard_map/reduce_scatter | solution.py:77
Sparse Core Ops, SparseCore 0:
  8.9 640.4 all-gather.1
  1279.1 148.9 reduce-scatter.2
  1430.5 19.2 reduce-scatter.4
where the time goes:
time: 1470 us; the launch traced here: 1460 us
  waiting for transfers between devices  804 us (55%)
  local copies, waits for them, and re-layouts  373 us (25%)
  other arithmetic  168 us (11%)
  matrix products  100 us (7%)
    all_gather x1, waiting for transfers between devices, on_device(): whole = lax.all_gather(pair_density, 'ka', axis=1, tiled=True)  633 us
    convert_element_type x3, local copies, waits for them, and re-layouts, on_device(): product = weight[..., None] * rotated[None].astype(jnp.float32)  190 us
    reduce_scatter x1, waiting for transfers between devices, on_device(): lax.psum_scatter(partial_value, 'ka', scatter_dimension=2, tiled=True)  149 us
    dot_general x1, matrix products, rotate_batch(): jnp.einsum('krbi,kboi->krbo', shaped, onehot, preferred_element_type=jnp....  56.6 us
    gather x5, local copies, waits for them, and re-layouts, on_device(): picked = jnp.take(whole, stars, axis=0)  54.2 us
    another operation x1, local copies, waits for them, and re-layouts, on_device(): row_part = flat.reshape(pair_rows, band_count, ga_count, slab)  50 us
    dot_general x1, matrix products, on_device(): jnp.einsum('rg,sfrh->fgh', row_part, flat_scaled, preferred_element_type=...  43.7 us
    convert_element_type x1, other arithmetic, on_device(): scaled_lo = (product - hi_back).astype(jnp.bfloat16)  42.4 us
  transfers between devices with their start and end apart: 3, of which 3 were waited for; matrix products, arithmetic and copies ran while one was open for 1% of the time, Pallas kernels for 0%

commit v1 on v0

v1 whole, which is shorter than its diff:
```python
import functools
import itertools

import jax
import jax.numpy as jnp
from jax import lax
from jax.experimental import pallas as pl
from jax.experimental.pallas import tpu as pltpu
from jax.sharding import PartitionSpec as P

NV = 8
NG = 2048
GB = 128
KI = 8
KF = 64
BLOCKS = NG // GB
NT = (((1,), (1,)), ((), ()))


def partial_kernel(rows, ct, chunk, bands, gas, star_ref, pd_ref, inv_ref, w_ref, out_ref, rot_ref):
    tile = pl.program_id(0)
    group = max(1, GB // rows)
    wide = group * rows

    @pl.when(tile == 0)
    def rotate():
        targets = lax.broadcasted_iota(jnp.int32, (GB, GB), 0)

        def one_eight(e, carry):
            for sub, b in itertools.product(range(8 // group), range(BLOCKS)):
                start = pl.multiple_of(e * (8 * rows) + sub * wide, wide)
                cols = slice(b * GB, (b + 1) * GB)
                moved = None
                source = inv_ref[pl.ds(pl.multiple_of(e * 8, 8), 8), cols]
                pieces = [pd_ref[star_ref[e * 8 + sub * group + m], :, cols] for m in range(group)]
                for m in range(group):
                    at = sub * group + m
                    if group == 1:
                        x = pieces[0]
                    else:
                        x = jnp.concatenate(
                            [p if n == m else jnp.zeros_like(p) for n, p in enumerate(pieces)], axis=0
                        )
                    onehot = jnp.where(
                        source[at : at + 1] == targets, 1.0, 0.0
                    ).astype(jnp.bfloat16)
                    part = lax.dot_general(onehot, x, NT, preferred_element_type=jnp.float32)
                    moved = part if moved is None else moved + part
                rot_ref[cols, pl.ds(start, wide)] = moved.astype(jnp.bfloat16)
            return carry

        lax.fori_loop(0, KF // 8, one_eight, 0)

    slab = NG // (bands * gas)
    ga = lax.axis_index("ga")
    base = pl.multiple_of(tile * ct, ct)
    out_ref[...] = jnp.zeros_like(out_ref)

    def one_chunk(q, carry):
        ks = pl.ds(pl.multiple_of(q * chunk, chunk), chunk)
        scaled = (rot_ref[pl.ds(base, ct), ks].astype(jnp.float32) * w_ref[:, ks]).astype(jnp.bfloat16)
        for band in range(bands):
            left = rot_ref[pl.ds(pl.multiple_of((band * gas + ga) * slab, slab), slab), ks]
            out_ref[band * slab : (band + 1) * slab, :] += lax.dot_general(
                left, scaled, NT, preferred_element_type=jnp.float32
            )
        return carry

    lax.fori_loop(0, (KF * rows) // chunk, one_chunk, 0)


def on_device(
    pair_density, valence_energy, conduction_energy, star_map, op_of_k, perm_lists, cond_top
):
    bands = lax.axis_size("band")
    gas = lax.axis_size("ga")
    piece = pair_density.shape[1]
    rows = piece * NV
    first = (lax.axis_index("ka") * bands + lax.axis_index("band")) * piece
    local = perm_lists.reshape(-1, BLOCKS, GB) - (jnp.arange(BLOCKS, dtype=jnp.int32) * GB)[None, :, None]
    hit = local[:, :, :, None] == jnp.arange(GB, dtype=jnp.int32)
    inverse = jnp.sum(jnp.where(hit, jnp.arange(GB, dtype=jnp.int32)[:, None], 0), axis=2)
    inv_k = jnp.take(inverse.reshape(-1, NG), op_of_k, axis=0)
    cond_own = lax.dynamic_slice_in_dim(conduction_energy, first, piece, 1)
    diff = jnp.take(valence_energy, star_map, axis=0)[:, None, :] - jnp.take(cond_own, star_map, axis=0)[:, :, None]
    mask = ((first + jnp.arange(piece))[None, :] < cond_top[:, None]).astype(jnp.float32)[:, :, None]
    weight = 4.0 / KF * diff / (diff * diff) * mask
    w_row = weight.reshape(1, KF * rows)

    ct, chunk = 256, min(2048, KF * rows)
    mine = NG // gas
    partial_chi = pl.pallas_call(
        functools.partial(partial_kernel, rows, ct, chunk, bands, gas),
        grid_spec=pltpu.PrefetchScalarGridSpec(
            num_scalar_prefetch=1,
            grid=(NG // ct,),
            in_specs=[pl.BlockSpec(memory_space=pltpu.VMEM)] * 3,
            out_specs=pl.BlockSpec((mine, ct), lambda j, s: (0, j)),
            scratch_shapes=[pltpu.VMEM((NG, KF * rows), jnp.bfloat16)],
        ),
        out_shape=jax.ShapeDtypeStruct((mine, NG), jnp.float32),
        compiler_params=pltpu.CompilerParams(vmem_limit_bytes=56 * 1024 * 1024),
    )(star_map, pair_density.reshape(KI, rows, NG), inv_k, w_row)
    column_sums = lax.psum_scatter(partial_chi, "ka", scatter_dimension=1, tiled=True)
    return lax.psum_scatter(column_sums, "band", scatter_dimension=0, tiled=True)[None]


def solution(mesh):
    return jax.shard_map(
        on_device,
        mesh=mesh,
        in_specs=(P(None, ("ka", "band"), None, None), P(), P(), P(), P(), P(), P()),
        out_specs=P(None, ("band", "ga"), "ka"),
        check_vma=False,
    )
```

time: 1470 us -> 286 us (0.19)
  waiting for transfers between devices: 804 us -> 174 us
  local copies, waits for them, and re-layouts: 373 us -> 4.89 us
  other arithmetic: 168 us -> 21.7 us
  matrix products: 100 us -> 0 us
  Pallas kernels: 0 us -> 71.5 us
    all_gather x1 -> x0, waiting for transfers between devices: 633 us -> none  [on_device(): whole = lax.all_gather(pair_density, 'ka', axis=1, tiled=True)]
    convert_element_type x4 -> x1, local copies, waits for them, and re-layouts: 221 us -> 0.09 us  [on_device(): ((first + jnp.arange(piece))[None, :] < cond_top[:, None]).astype(jnp.flo...]
    dot_general x2 -> x0, matrix products: 100 us -> none  [the longest x1 56.6 us: rotate_batch(): jnp.einsum('krbi,kboi->krbo', shaped, onehot, preferred_element_type=jnp....]
    convert_element_type x3 -> x1, other arithmetic: 74.8 us -> 0.73 us  [on_device(): ((first + jnp.arange(piece))[None, :] < cond_top[:, None]).astype(jnp.flo...]
    pallas_call x0 -> x1, Pallas kernels: none -> 71.5 us  [on_device(): pl.pallas_call(functools.partial(partial_kernel, rows, ct, chunk, bands,...]
    gather x11 -> x3, local copies, waits for them, and re-layouts: 60.4 us -> 2.63 us  [the longest x1 1.28 us: on_device(): jnp.take(valence_energy, star_map, axis=0)[:, None, :]]
    another operation x1 -> x0, local copies, waits for them, and re-layouts: 50 us -> none  [on_device(): row_part = flat.reshape(pair_rows, band_count, ga_count, slab)]
    another operation x1 -> x0, other arithmetic: 32.5 us -> none  [on_device(): jnp.stack([scaled_hi.reshape(NF, pair_rows, NG), scaled_lo.reshape(NF, pa...]
  transfers between devices with their start and end apart: 3 -> 2, of which waited for: 3 -> 2; matrix products, arithmetic and copies ran while one was open for 1% -> 0% of each run, Pallas kernels for 0% -> 0%
where the time goes in v1:
time: 286 us; the launch traced here: 285 us
  waiting for transfers between devices  174 us (61%)
  Pallas kernels  71.5 us (25%)
  other arithmetic  21.7 us (8%)
  between operations  13.5 us (5%)
  local copies, waits for them, and re-layouts  4.89 us (2%)
    reduce_scatter x1, waiting for transfers between devices, on_device(): lax.psum_scatter(partial_chi, 'ka', scatter_dimension=1, tiled=True)  152 us
    pallas_call x1, Pallas kernels, on_device(): pl.pallas_call(functools.partial(partial_kernel, rows, ct, chunk, bands,...  71.5 us
    reduce_scatter x1, waiting for transfers between devices, on_device(): lax.psum_scatter(column_sums, 'band', scatter_dimension=0, tiled=True)[None]  21.6 us
    reduce_sum x1, other arithmetic, on_device(): jnp.sum(jnp.where(hit, jnp.arange(GB, dtype=jnp.int32)[:, None], 0), axis=2)  16.8 us
  transfers between devices with their start and end apart: 2, of which 2 were waited for; matrix products, arithmetic and copies ran while one was open for 0% of the time, Pallas kernels for 0%

profile of v1, /device:TPU:0, one launch (start us, length us, event | category | flops | bytes accessed | tf_op | source)
XLA Modules:
  0.0 285.4 jit_solution(14641797984782757231)
XLA Ops:
  6.5 0.0 copy-start
  6.5 0.0 reduce-scatter.3.cloned.1.call-start
  6.5 0.7 compare_and_fusion.1
  7.2 0.7 compare_select_fusion.1
  7.9 0.7 compare_and_fusion
  8.5 0.7 compare_select_fusion
  9.2 0.7 compare_convert_fusion
  9.9 0.1 copy.8
  10.0 0.0 copy-done
  10.0 0.1 constant_dynamic-slice_fusion
  10.1 0.6 gather_fusion.2
  10.7 1.3 gather_fusion.1
  12.0 0.1 broadcast_select_fusion.1
  12.1 0.1 broadcast_select_fusion.2
  12.1 1.1 copy.9
  13.2 0.1 bitcast_subtract_fusion
  13.3 16.8 %select_reduce_fusion = s32[48,16,128]{2,1,0:T(8,128)S(1)} fusion(s32[48,16,128]{2,1,0:T(8,128)S(1)} %bitcast_subtract_fusion), kind=kLoop, calls=%fused_computation.3 | loop fusion | flops 37650432 | bytes 786432 | tf_op jit(solution)/shard_map/reduce_sum | solution.py:82
  30.1 0.1 copy.12
  30.2 0.3 fusion.1
  30.6 0.9 mul.64.w_ref
  31.5 0.8 gather_fusion
  32.2 0.9 broadcast_select_fusion.inv_ref
  33.1 71.5 %shard_map.73 = f32[1024,2048]{1,0:T(8,128)} custom-call(s32[64]{0:T(128)} %star_ref.1, bf16[8,128,2048]{2,1,0:T(8,128)(2,1)} %bitcast.10, s32[64,2048]{1,0:T(8,128)} %broadcast_select_fusion.inv_ref, f32[1,8192]{1,0:T(1,128)} %mul.64.w_ref), custom_call_target="tpu_custom_call" | custom-call | tf_op jit(solution)/shard_map/pallas_call | solution.py:92
  104.6 0.0 reduce-scatter.3.cloned.1.call-update
  104.7 0.0 reduce-scatter.5.cloned.1.call-start
  104.7 152.2 %reduce-scatter.3.cloned.1.call-done = f32[1024,256]{1,0:T(8,128)} async-done(((f32[1024,2048]{1,0:T(8,128)}), f32[1024,256]{1,0:T(8,128)}) %reduce-scatter.3.cloned.1.call-update) | async-done | bytes 1048592 | tf_op jit(solution)/shard_map/reduce_scatter | solution.py:104
  256.9 0.0 reduce-scatter.5.cloned.1.call-update
  256.9 21.6 %reduce-scatter.5.cloned.1.call-done = f32[512,256]{1,0:T(8,128)} async-done(((f32[1024,256]{1,0:T(8,128)}), f32[512,256]{1,0:T(8,128)}) %reduce-scatter.5.cloned.1.call-update) | async-done | bytes 524304 | tf_op jit(solution)/shard_map/reduce_scatter | solution.py:105
  (4 shorter events, 0.0 us)
Async XLA Ops:
  6.5 3.5 %copy-start = (f32[8,256]{1,0:T(8,128)S(1)}, f32[8,256]{1,0:T(8,128)}, u32[]{:S(2)}) copy-start(f32[8,256]{1,0:T(8,128)} %param.9) | copy-start | bytes 24580
  6.5 250.4 %reduce-scatter.3.cloned.1.call-start = ((), (), s32[]{:S(2)}) async-start(), calls=%async_computation.2 | async-start | bytes 9437184 | tf_op jit(solution)/shard_map/reduce_scatter | solution.py:104
  104.7 173.9 %reduce-scatter.5.cloned.1.call-start = ((), (), s32[]{:S(2)}) async-start(), calls=%async_computation.3 | async-start | bytes 1572864 | tf_op jit(solution)/shard_map/reduce_scatter | solution.py:105
Sparse Core Ops, SparseCore 0:
  104.8 152.0 reduce-scatter.2
  259.2 19.2 reduce-scatter.4

commit v2 on v1

--- a/solution.py
+++ b/solution.py
@@ -17,39 +17,43 @@
 NT = (((1,), (1,)), ((), ()))
 
 
+def rotate_all(rows, star_ref, pd_ref, inv_ref, rot_ref):
+    group = max(1, GB // rows)
+    wide = group * rows
+    targets = lax.broadcasted_iota(jnp.int32, (GB, GB), 0)
+
+    def one_eight(e, carry):
+        for sub, b in itertools.product(range(8 // group), range(BLOCKS)):
+            start = pl.multiple_of(e * (8 * rows) + sub * wide, wide)
+            cols = slice(b * GB, (b + 1) * GB)
+            moved = None
+            source = inv_ref[pl.ds(pl.multiple_of(e * 8, 8), 8), cols]
+            pieces = [pd_ref[star_ref[e * 8 + sub * group + m], :, cols] for m in range(group)]
+            for m in range(group):
+                at = sub * group + m
+                if group == 1:
+                    x = pieces[0]
+                else:
+                    x = jnp.concatenate(
+                        [p if n == m else jnp.zeros_like(p) for n, p in enumerate(pieces)], axis=0
+                    )
+                onehot = jnp.where(
+                    source[at : at + 1] == targets, 1.0, 0.0
+                ).astype(jnp.bfloat16)
+                part = lax.dot_general(onehot, x, NT, preferred_element_type=jnp.float32)
+                moved = part if moved is None else moved + part
+            rot_ref[cols, pl.ds(start, wide)] = moved.astype(jnp.bfloat16)
+        return carry
+
+    lax.fori_loop(0, KF // 8, one_eight, 0)
+
+
 def partial_kernel(rows, ct, chunk, bands, gas, star_ref, pd_ref, inv_ref, w_ref, out_ref, rot_ref):
     tile = pl.program_id(0)
-    group = max(1, GB // rows)
-    wide = group * rows
 
     @pl.when(tile == 0)
     def rotate():
-        targets = lax.broadcasted_iota(jnp.int32, (GB, GB), 0)
-
-        def one_eight(e, carry):
-            for sub, b in itertools.product(range(8 // group), range(BLOCKS)):
-                start = pl.multiple_of(e * (8 * rows) + sub * wide, wide)
-                cols = slice(b * GB, (b + 1) * GB)
-                moved = None
-                source = inv_ref[pl.ds(pl.multiple_of(e * 8, 8), 8), cols]
-                pieces = [pd_ref[star_ref[e * 8 + sub * group + m], :, cols] for m in range(group)]
-                for m in range(group):
-                    at = sub * group + m
-                    if group == 1:
-                        x = pieces[0]
-                    else:
-                        x = jnp.concatenate(
-                            [p if n == m else jnp.zeros_like(p) for n, p in enumerate(pieces)], axis=0
-                        )
-                    onehot = jnp.where(
-                        source[at : at + 1] == targets, 1.0, 0.0
-                    ).astype(jnp.bfloat16)
-                    part = lax.dot_general(onehot, x, NT, preferred_element_type=jnp.float32)
-                    moved = part if moved is None else moved + part
-                rot_ref[cols, pl.ds(start, wide)] = moved.astype(jnp.bfloat16)
-            return carry
-
-        lax.fori_loop(0, KF // 8, one_eight, 0)
+        rotate_all(rows, star_ref, pd_ref, inv_ref, rot_ref)
 
     slab = NG // (bands * gas)
     ga = lax.axis_index("ga")
@@ -67,6 +71,119 @@
         return carry
 
     lax.fori_loop(0, (KF * rows) // chunk, one_chunk, 0)
+
+
+def send(source, target, out_sem, in_sem, device):
+    return pltpu.make_async_remote_copy(
+        src_ref=source,
+        dst_ref=target,
+        send_sem=out_sem,
+        recv_sem=in_sem,
+        device_id=device,
+        device_id_type=pl.DeviceIdType.MESH,
+    )
+
+
+STEPS_Z = (2, 3, 1, 0)
+
+
+def fused_kernel(
+    rows, chunk, star_ref, pd_ref, inv_ref, w_ref, out_ref,
+    rot_ref, acc, x_out, x_in, y_out, y_in, z_in,
+    xs_sem, xr_sem, ys_sem, yr_sem, zs_sem, zr_sem,
+):
+    ka = lax.axis_index("ka")
+    x = lax.axis_index("band")
+    ga = lax.axis_index("ga")
+    z, y = ka // 2, ka % 2
+    to_x = {"band": 1 - x}
+    to_y = {"ka": z * 2 + (1 - y)}
+    to_z = [{"ka": ((z + step) % 4) * 2 + y} for step in STEPS_Z[:3]]
+    barrier = pltpu.get_barrier_semaphore()
+    for device in [to_x, to_y] + to_z:
+        pl.semaphore_signal(barrier, inc=1, device_id=device, device_id_type=pl.DeviceIdType.MESH)
+    pl.semaphore_wait(barrier, 5)
+
+    rotate_all(rows, star_ref, pd_ref, inv_ref, rot_ref)
+
+    slab, ct = out_ref.shape
+    own_rows = pl.ds(pl.multiple_of((x * 2 + ga) * slab, slab), slab)
+    far_rows = pl.ds(pl.multiple_of(((1 - x) * 2 + ga) * slab, slab), slab)
+
+    def compute(t, z_to, y_to):
+        base = pl.multiple_of((z_to * 2 + y_to) * ct, ct)
+        acc[t] = jnp.zeros((slab, ct), jnp.float32)
+        out_ref[...] = jnp.zeros((slab, ct), jnp.float32)
+
+        def one_chunk(q, carry):
+            ks = pl.ds(pl.multiple_of(q * chunk, chunk), chunk)
+            scaled = (rot_ref[pl.ds(base, ct), ks].astype(jnp.float32) * w_ref[:, ks]).astype(jnp.bfloat16)
+            out_ref[...] += lax.dot_general(rot_ref[far_rows, ks], scaled, NT, preferred_element_type=jnp.float32)
+            acc[t] += lax.dot_general(rot_ref[own_rows, ks], scaled, NT, preferred_element_type=jnp.float32)
+            return carry
+
+        lax.fori_loop(0, (KF * rows) // chunk, one_chunk, 0)
+        x_out[t] = out_ref[...].astype(jnp.bfloat16)
+
+    x_copies = [send(x_out.at[t], x_in.at[t], xs_sem.at[t], xr_sem.at[t], to_x) for t in range(8)]
+    y_copies = [send(y_out.at[i], y_in.at[i], ys_sem.at[i], yr_sem.at[i], to_y) for i in range(4)]
+    z_copies = [send(acc.at[2 * i + 1], z_in.at[i], zs_sem.at[i], zr_sem.at[i], to_z[i]) for i in range(3)]
+
+    def take_x(t):
+        x_copies[t].wait_recv()
+        acc[t] += x_in[t].astype(jnp.float32)
+        if t % 2 == 0:
+            y_out[t // 2] = acc[t].astype(jnp.bfloat16)
+            y_copies[t // 2].start()
+
+    def take_y(i):
+        y_copies[i].wait_recv()
+        acc[2 * i + 1] += y_in[i].astype(jnp.float32)
+        if i < 3:
+            z_copies[i].start()
+
+    for t in range(8):
+        i = t // 2
+        compute(t, (z + STEPS_Z[i]) % 4, (1 - y) if t % 2 == 0 else y)
+        x_copies[t].start()
+        if t >= 1:
+            take_x(t - 1)
+            if t >= 3 and t % 2 == 1:
+                take_y(i - 1)
+    take_x(7)
+    take_y(3)
+    total = acc[7]
+    for i in range(3):
+        z_copies[i].wait_recv()
+        total += z_in[i]
+    out_ref[...] = total
+    for copy in x_copies + y_copies + z_copies:
+        copy.wait_send()
+
+
+def fused(rows, star_map, pd, inv_k, w_row):
+    slab, ct = 512, 256
+    f32, bf16 = jnp.float32, jnp.bfloat16
+    dma = pltpu.SemaphoreType.DMA
+    return pl.pallas_call(
+        functools.partial(fused_kernel, rows, 2048),
+        in_specs=[pl.BlockSpec(memory_space=pltpu.SMEM)] + [pl.BlockSpec(memory_space=pltpu.VMEM)] * 3,
+        out_specs=pl.BlockSpec(memory_space=pltpu.VMEM),
+        out_shape=jax.ShapeDtypeStruct((slab, ct), f32),
+        scratch_shapes=[
+            pltpu.VMEM((NG, KF * rows), bf16),
+            pltpu.VMEM((8, slab, ct), f32),
+            pltpu.VMEM((8, slab, ct), bf16),
+            pltpu.VMEM((8, slab, ct), bf16),
+            pltpu.VMEM((4, slab, ct), bf16),
+            pltpu.VMEM((4, slab, ct), bf16),
+            pltpu.VMEM((3, slab, ct), f32),
+            dma((8,)), dma((8,)), dma((4,)), dma((4,)), dma((3,)), dma((3,)),
+        ],
+        compiler_params=pltpu.CompilerParams(
+            collective_id=0, has_side_effects=True, vmem_limit_bytes=60 * 1024 * 1024
+        ),
+    )(star_map, pd, inv_k, w_row)
 
 
 def on_device(
@@ -87,6 +204,8 @@
     weight = 4.0 / KF * diff / (diff * diff) * mask
     w_row = weight.reshape(1, KF * rows)
 
+    if (lax.axis_size("ka"), bands, gas) == (8, 2, 2):
+        return fused(rows, star_map, pair_density.reshape(KI, rows, NG), inv_k, w_row)[None]
     ct, chunk = 256, min(2048, KF * rows)
     mine = NG // gas
     partial_chi = pl.pallas_call(

time: 286 us -> 130 us (0.45)
  waiting for transfers between devices: 174 us -> 0 us
  Pallas kernels: 71.5 us -> 102 us
  between operations: 13.5 us -> 0.09 us
    reduce_scatter x2 -> x0, waiting for transfers between devices: 174 us -> none  [the longest x1 152 us: on_device(): lax.psum_scatter(partial_chi, 'ka', scatter_dimension=1, tiled=True)]
    pallas_call x1, Pallas kernels: 71.5 us -> 102 us  [fused(): pl.pallas_call(functools.partial(fused_kernel, rows, 2048), in_specs=[pl....]
  transfers between devices with their start and end apart: 2 -> 0, of which waited for: 2 -> 0; matrix products, arithmetic and copies ran while one was open for 0% -> 0% of each run, Pallas kernels for 0% -> 0%
where the time goes in v2:
time: 130 us
  Pallas kernels  102 us (78%)
  other arithmetic  20.3 us (16%)
  local copies, waits for them, and re-layouts  7.45 us (6%)
    pallas_call x1, Pallas kernels, fused(): pl.pallas_call(functools.partial(fused_kernel, rows, 2048), in_specs=[pl....  102 us
    reduce_sum x1, other arithmetic, on_device(): jnp.sum(jnp.where(hit, jnp.arange(GB, dtype=jnp.int32)[:, None], 0), axis=2)  16.8 us
    unnamed x7, local copies, waits for them, and re-layouts  3.76 us

profile of v2, /device:TPU:0, one launch (start us, length us, event | category | flops | bytes accessed | tf_op | source)
XLA Modules:
  0.0 130.1 jit_solution(3756776565741953904)
XLA Ops:
  0.0 0.0 copy-start
  0.0 0.0 copy-start.1
  0.0 0.7 copy-done
  0.7 0.1 constant_dynamic-slice_fusion
  0.8 0.7 compare_select_fusion
  1.4 0.6 gather_fusion.2
  2.0 0.7 compare_and_fusion
  2.7 0.1 broadcast_select_fusion.1
  2.8 0.7 compare_convert_fusion
  3.5 0.1 copy.8
  3.6 1.3 gather_fusion.1
  4.9 0.1 broadcast_select_fusion.2
  5.0 0.3 fusion.1
  5.3 0.9 mul.64.w_ref
  6.2 1.1 copy.9
  7.3 0.1 bitcast_subtract_fusion
  7.4 16.8 %select_reduce_fusion = s32[48,16,128]{2,1,0:T(8,128)S(1)} fusion(s32[48,16,128]{2,1,0:T(8,128)S(1)} %bitcast_subtract_fusion), kind=kLoop, calls=%fused_computation.3 | loop fusion | flops 37650432 | bytes 786432 | tf_op jit(solution)/shard_map/reduce_sum | solution.py:199
  24.2 0.1 copy.12
  24.3 0.0 copy-done.1
  24.3 0.8 gather_fusion
  25.1 0.9 broadcast_select_fusion.inv_ref
  26.0 102.2 %shard_map.73 = f32[512,256]{1,0:T(8,128)} custom-call(s32[64]{0:T(128)} %star_ref.1, bf16[8,128,2048]{2,1,0:T(8,128)(2,1)} %bitcast.10, s32[64,2048]{1,0:T(8,128)} %broadcast_select_fusion.inv_ref, f32[1,8192]{1,0:T(1,128)} %mul.64.w_ref), custom_call_target="tpu_custom_call" | custom-call | tf_op jit(solution)/shard_map/pallas_call | solution.py:168
  128.2 1.9 %copy.14 = f32[1,512,256]{2,1,0:T(8,128)} copy(f32[1,512,256]{2,1,0:T(8,128)} %bitcast.11) | data formatting | bytes 1048576
  (6 shorter events, 0.0 us)
Async XLA Ops:
  0.0 0.7 copy-start
  0.0 24.3 %copy-start.1 = (s32[64]{0:T(128)S(1)}, s32[64]{0:T(128)}, u32[]{:S(2)}) copy-start(s32[64]{0:T(128)} %param.11) | copy-start | bytes 772

commit v3 on v2

--- a/solution.py
+++ b/solution.py
@@ -1,5 +1,4 @@
 import functools
-import itertools
 
 import jax
 import jax.numpy as jnp
@@ -17,43 +16,43 @@
 NT = (((1,), (1,)), ((), ()))
 
 
-def rotate_all(rows, star_ref, pd_ref, inv_ref, rot_ref):
+PAIR = GB // KF
+
+
+def rotate_tile(rows, tile, star_ref, pd_ref, perm_ref, rot_ref):
     group = max(1, GB // rows)
     wide = group * rows
-    targets = lax.broadcasted_iota(jnp.int32, (GB, GB), 0)
-
-    def one_eight(e, carry):
-        for sub, b in itertools.product(range(8 // group), range(BLOCKS)):
-            start = pl.multiple_of(e * (8 * rows) + sub * wide, wide)
-            cols = slice(b * GB, (b + 1) * GB)
+    slots = lax.broadcasted_iota(jnp.int32, (GB, GB), 1)
+    source = perm_ref[:, pl.ds(pl.multiple_of(tile * GB, GB), GB)]
+    for half in range(PAIR):
+        cols = pl.ds(pl.multiple_of((tile * PAIR + half) * GB, GB), GB)
+        for q in range(KF // group):
             moved = None
-            source = inv_ref[pl.ds(pl.multiple_of(e * 8, 8), 8), cols]
-            pieces = [pd_ref[star_ref[e * 8 + sub * group + m], :, cols] for m in range(group)]
+            pieces = [pd_ref[star_ref[q * group + m], :, cols] for m in range(group)]
             for m in range(group):
-                at = sub * group + m
+                lane = half * KF + q * group + m
                 if group == 1:
                     x = pieces[0]
                 else:
                     x = jnp.concatenate(
                         [p if n == m else jnp.zeros_like(p) for n, p in enumerate(pieces)], axis=0
                     )
-                onehot = jnp.where(
-                    source[at : at + 1] == targets, 1.0, 0.0
-                ).astype(jnp.bfloat16)
+                onehot = jnp.where(source[:, lane : lane + 1] == slots, 1.0, 0.0).astype(jnp.bfloat16)
                 part = lax.dot_general(onehot, x, NT, preferred_element_type=jnp.float32)
                 moved = part if moved is None else moved + part
-            rot_ref[cols, pl.ds(start, wide)] = moved.astype(jnp.bfloat16)
-        return carry
-
-    lax.fori_loop(0, KF // 8, one_eight, 0)
-
-
-def partial_kernel(rows, ct, chunk, bands, gas, star_ref, pd_ref, inv_ref, w_ref, out_ref, rot_ref):
+            rot_ref[cols, q * wide : (q + 1) * wide] = moved.astype(jnp.bfloat16)
+
+
+def partial_kernel(rows, ct, chunk, bands, gas, star_ref, pd_ref, perm_ref, w_ref, out_ref, rot_ref):
     tile = pl.program_id(0)
 
     @pl.when(tile == 0)
     def rotate():
-        rotate_all(rows, star_ref, pd_ref, inv_ref, rot_ref)
+        def one(i, carry):
+            rotate_tile(rows, i, star_ref, pd_ref, perm_ref, rot_ref)
+            return carry
+
+        lax.fori_loop(0, BLOCKS // PAIR, one, 0)
 
     slab = NG // (bands * gas)
     ga = lax.axis_index("ga")
@@ -85,11 +84,12 @@
 
 
 STEPS_Z = (2, 3, 1, 0)
+ORDER = (0, 1, 2, 4, 3, 6, 5, 7)
 
 
 def fused_kernel(
-    rows, chunk, star_ref, pd_ref, inv_ref, w_ref, out_ref,
-    rot_ref, acc, x_out, x_in, y_out, y_in, z_in,
+    rows, chunk, star_ref, pd_ref, perm_ref, w_ref, out_ref,
+    rot_ref, acc, x_out, x_in, y_in, z_in,
     xs_sem, xr_sem, ys_sem, yr_sem, zs_sem, zr_sem,
 ):
     ka = lax.axis_index("ka")
@@ -104,7 +104,18 @@
         pl.semaphore_signal(barrier, inc=1, device_id=device, device_id_type=pl.DeviceIdType.MESH)
     pl.semaphore_wait(barrier, 5)
 
-    rotate_all(rows, star_ref, pd_ref, inv_ref, rot_ref)
+    def rotate_pair(z_of):
+        def one(i, carry):
+            rotate_tile(rows, z_of * 2 + i, star_ref, pd_ref, perm_ref, rot_ref)
+            return carry
+
+        lax.fori_loop(0, 2, one, 0)
+
+    def row_tile(i, carry):
+        rotate_tile(rows, (i // 2) * 4 + ga * 2 + i % 2, star_ref, pd_ref, perm_ref, rot_ref)
+        return carry
+
+    lax.fori_loop(0, 4, row_tile, 0)
 
     slab, ct = out_ref.shape
     own_rows = pl.ds(pl.multiple_of((x * 2 + ga) * slab, slab), slab)
@@ -126,32 +137,41 @@
         x_out[t] = out_ref[...].astype(jnp.bfloat16)
 
     x_copies = [send(x_out.at[t], x_in.at[t], xs_sem.at[t], xr_sem.at[t], to_x) for t in range(8)]
-    y_copies = [send(y_out.at[i], y_in.at[i], ys_sem.at[i], yr_sem.at[i], to_y) for i in range(4)]
+    y_copies = [send(acc.at[2 * i], y_in.at[i], ys_sem.at[i], yr_sem.at[i], to_y) for i in range(4)]
     z_copies = [send(acc.at[2 * i + 1], z_in.at[i], zs_sem.at[i], zr_sem.at[i], to_z[i]) for i in range(3)]
 
     def take_x(t):
         x_copies[t].wait_recv()
         acc[t] += x_in[t].astype(jnp.float32)
         if t % 2 == 0:
-            y_out[t // 2] = acc[t].astype(jnp.bfloat16)
             y_copies[t // 2].start()
 
     def take_y(i):
         y_copies[i].wait_recv()
-        acc[2 * i + 1] += y_in[i].astype(jnp.float32)
+        acc[2 * i + 1] += y_in[i]
         if i < 3:
             z_copies[i].start()
 
-    for t in range(8):
+    before, rotated, summed = None, set(), []
+    for t in ORDER:
         i = t // 2
-        compute(t, (z + STEPS_Z[i]) % 4, (1 - y) if t % 2 == 0 else y)
+        z_of = (z + STEPS_Z[i]) % 4
+        if i not in rotated:
+            rotated.add(i)
+            pl.when(z_of % 2 != ga)(functools.partial(rotate_pair, z_of))
+        compute(t, z_of, (1 - y) if t % 2 == 0 else y)
         x_copies[t].start()
-        if t >= 1:
-            take_x(t - 1)
-            if t >= 3 and t % 2 == 1:
-                take_y(i - 1)
-    take_x(7)
-    take_y(3)
+        if summed:
+            take_y(summed.pop(0))
+        if before is not None:
+            take_x(before)
+            if before % 2 == 1:
+                summed.append(before // 2)
+        before = t
+    for i in summed:
+        take_y(i)
+    take_x(before)
+    take_y(before // 2)
     total = acc[7]
     for i in range(3):
         z_copies[i].wait_recv()
@@ -161,7 +181,7 @@
         copy.wait_send()
 
 
-def fused(rows, star_map, pd, inv_k, w_row):
+def fused(rows, star_map, pd, perm_k, w_row):
     slab, ct = 512, 256
     f32, bf16 = jnp.float32, jnp.bfloat16
     dma = pltpu.SemaphoreType.DMA
@@ -175,15 +195,14 @@
             pltpu.VMEM((8, slab, ct), f32),
             pltpu.VMEM((8, slab, ct), bf16),
             pltpu.VMEM((8, slab, ct), bf16),
-            pltpu.VMEM((4, slab, ct), bf16),
-            pltpu.VMEM((4, slab, ct), bf16),
+            pltpu.VMEM((4, slab, ct), f32),
             pltpu.VMEM((3, slab, ct), f32),
             dma((8,)), dma((8,)), dma((4,)), dma((4,)), dma((3,)), dma((3,)),
         ],
         compiler_params=pltpu.CompilerParams(
             collective_id=0, has_side_effects=True, vmem_limit_bytes=60 * 1024 * 1024
         ),
-    )(star_map, pd, inv_k, w_row)
+    )(star_map, pd, perm_k, w_row)
 
 
 def on_device(
@@ -194,10 +213,9 @@
     piece = pair_density.shape[1]
     rows = piece * NV
     first = (lax.axis_index("ka") * bands + lax.axis_index("band")) * piece
-    local = perm_lists.reshape(-1, BLOCKS, GB) - (jnp.arange(BLOCKS, dtype=jnp.int32) * GB)[None, :, None]
-    hit = local[:, :, :, None] == jnp.arange(GB, dtype=jnp.int32)
-    inverse = jnp.sum(jnp.where(hit, jnp.arange(GB, dtype=jnp.int32)[:, None], 0), axis=2)
-    inv_k = jnp.take(inverse.reshape(-1, NG), op_of_k, axis=0)
+    local = jnp.take(perm_lists.reshape(-1, BLOCKS, GB), op_of_k, axis=0)
+    local = local - (jnp.arange(BLOCKS, dtype=jnp.int32) * GB)[None, :, None]
+    perm_k = local.transpose(2, 1, 0).reshape(GB, BLOCKS * KF)
     cond_own = lax.dynamic_slice_in_dim(conduction_energy, first, piece, 1)
     diff = jnp.take(valence_energy, star_map, axis=0)[:, None, :] - jnp.take(cond_own, star_map, axis=0)[:, :, None]
     mask = ((first + jnp.arange(piece))[None, :] < cond_top[:, None]).astype(jnp.float32)[:, :, None]
@@ -205,7 +223,7 @@
     w_row = weight.reshape(1, KF * rows)
 
     if (lax.axis_size("ka"), bands, gas) == (8, 2, 2):
-        return fused(rows, star_map, pair_density.reshape(KI, rows, NG), inv_k, w_row)[None]
+        return fused(rows, star_map, pair_density.reshape(KI, rows, NG), perm_k, w_row)[None]
     ct, chunk = 256, min(2048, KF * rows)
     mine = NG // gas
     partial_chi = pl.pallas_call(
@@ -219,7 +237,7 @@
         ),
         out_shape=jax.ShapeDtypeStruct((mine, NG), jnp.float32),
         compiler_params=pltpu.CompilerParams(vmem_limit_bytes=56 * 1024 * 1024),
-    )(star_map, pair_density.reshape(KI, rows, NG), inv_k, w_row)
+    )(star_map, pair_density.reshape(KI, rows, NG), perm_k, w_row)
     column_sums = lax.psum_scatter(partial_chi, "ka", scatter_dimension=1, tiled=True)
     return lax.psum_scatter(column_sums, "band", scatter_dimension=0, tiled=True)[None]
 

time: 130 us -> 106 us (0.82)
  other arithmetic: 20.3 us -> 4.04 us
  Pallas kernels: 102 us -> 93.3 us
    reduce_sum x1 -> x0, other arithmetic: 16.8 us -> none  [on_device(): jnp.sum(jnp.where(hit, jnp.arange(GB, dtype=jnp.int32)[:, None], 0), axis=2)]
    pallas_call x1, Pallas kernels: 102 us -> 93.3 us  [fused(): pl.pallas_call(functools.partial(fused_kernel, rows, 2048), in_specs=[pl....]
    unnamed x7 -> x4, local copies, waits for them, and re-layouts: 3.76 us -> 3.63 us
where the time goes in v3:
time: 106 us
  Pallas kernels  93.3 us (88%)
  local copies, waits for them, and re-layouts  8.37 us (8%)
  other arithmetic  4.04 us (4%)
    pallas_call x1, Pallas kernels, fused(): pl.pallas_call(functools.partial(fused_kernel, rows, 2048), in_specs=[pl....  93.3 us
    unnamed x4, local copies, waits for them, and re-layouts  3.63 us

profile of v3, /device:TPU:0, one launch (start us, length us, event | category | flops | bytes accessed | tf_op | source)
XLA Modules:
  0.0 105.8 jit_solution(11212990569939968280)
XLA Ops:
  0.0 0.0 copy-start
  0.0 0.7 copy-done
  0.7 0.1 constant_dynamic-slice_fusion
  0.8 0.7 compare_select_fusion
  1.4 0.6 gather_fusion.2
  2.0 0.7 compare_and_fusion
  2.7 0.1 broadcast_select_fusion
  2.8 0.7 compare_convert_fusion
  3.5 0.1 copy.11
  3.6 1.3 %gather_fusion.1 = f32[64,8]{1,0:T(8,128)S(1)} fusion(f32[8,8]{1,0:T(8,128)} %param.8, s32[1024]{0:T(1024)S(1)} %pad_clamp_fusion), kind=kCustom, calls=%fused_computation.1 | custom fusion | bytes 4352 | tf_op jit(solution)/shard_map/jit(_take)/gather | solution.py:220
  4.9 0.1 broadcast_select_fusion.1
  5.0 0.3 fusion.1
  5.3 0.9 mul.64.w_ref
  6.2 1.1 %copy.13 = s32[6,8,16,128]{3,2,1,0:T(8,128)S(1)} copy(s32[6,8,16,128]{3,1,2,0:T(8,128)} %bitcast.11) | data formatting | bytes 786432
  7.3 0.7 compare_select_fusion.1
  7.9 0.6 gather_fusion
  8.6 0.7 compare_and_fusion.1
  9.3 0.2 subtract_bitcast_fusion
  9.4 0.2 copy.10
  9.6 1.0 copy.12.perm_ref
  10.6 93.3 %shard_map.73 = f32[512,256]{1,0:T(8,128)} custom-call(s32[64]{0:T(128)} %star_ref.1, bf16[8,128,2048]{2,1,0:T(8,128)(2,1)} %bitcast.7, s32[128,1024]{1,0:T(8,128)} %copy.12.perm_ref, f32[1,8192]{1,0:T(1,128)} %mul.64.w_ref), custom_call_target="tpu_custom_call" | custom-call | tf_op jit(solution)/shard_map/pallas_call | solution.py:188
  103.9 1.9 %copy.15 = f32[1,512,256]{2,1,0:T(8,128)} copy(f32[1,512,256]{2,1,0:T(8,128)} %bitcast.10) | data formatting | bytes 1048576
  (4 shorter events, 0.0 us)
Async XLA Ops:
  0.0 0.7 copy-start

commit v4 on v3

--- a/solution.py
+++ b/solution.py
@@ -186,7 +186,7 @@
     f32, bf16 = jnp.float32, jnp.bfloat16
     dma = pltpu.SemaphoreType.DMA
     return pl.pallas_call(
-        functools.partial(fused_kernel, rows, 2048),
+        functools.partial(fused_kernel, rows, min(4096, KF * rows)),
         in_specs=[pl.BlockSpec(memory_space=pltpu.SMEM)] + [pl.BlockSpec(memory_space=pltpu.VMEM)] * 3,
         out_specs=pl.BlockSpec(memory_space=pltpu.VMEM),
         out_shape=jax.ShapeDtypeStruct((slab, ct), f32),

time: 106 us -> 105 us (level)
  no operation moved by 1% of the time
where the time goes in v4:
time: 105 us
  Pallas kernels  92.5 us (88%)
  local copies, waits for them, and re-layouts  8.37 us (8%)
  other arithmetic  4.04 us (4%)
    pallas_call x1, Pallas kernels, fused(): pl.pallas_call(functools.partial(fused_kernel, rows, min(4096, KF * rows)...  92.5 us
    unnamed x4, local copies, waits for them, and re-layouts  3.63 us

profile of v4, /device:TPU:0, one launch (start us, length us, event | category | flops | bytes accessed | tf_op | source)
XLA Modules:
  0.0 105.0 jit_solution(7125080278852981789)
XLA Ops:
  0.0 0.0 copy-start
  0.0 0.7 copy-done
  0.7 0.1 constant_dynamic-slice_fusion
  0.8 0.7 compare_select_fusion
  1.4 0.6 gather_fusion.2
  2.0 0.7 compare_and_fusion
  2.7 0.1 broadcast_select_fusion
  2.8 0.7 compare_convert_fusion
  3.5 0.1 copy.11
  3.6 1.3 %gather_fusion.1 = f32[64,8]{1,0:T(8,128)S(1)} fusion(f32[8,8]{1,0:T(8,128)} %param.8, s32[1024]{0:T(1024)S(1)} %pad_clamp_fusion), kind=kCustom, calls=%fused_computation.1 | custom fusion | bytes 4352 | tf_op jit(solution)/shard_map/jit(_take)/gather | solution.py:220
  4.9 0.1 broadcast_select_fusion.1
  5.0 0.3 fusion.1
  5.3 0.9 mul.64.w_ref
  6.2 1.1 %copy.13 = s32[6,8,16,128]{3,2,1,0:T(8,128)S(1)} copy(s32[6,8,16,128]{3,1,2,0:T(8,128)} %bitcast.11) | data formatting | bytes 786432
  7.3 0.7 compare_select_fusion.1
  7.9 0.6 gather_fusion
  8.6 0.7 compare_and_fusion.1
  9.3 0.2 subtract_bitcast_fusion
  9.4 0.2 copy.10
  9.6 1.0 copy.12.perm_ref
  10.6 92.5 %shard_map.73 = f32[512,256]{1,0:T(8,128)} custom-call(s32[64]{0:T(128)} %star_ref.1, bf16[8,128,2048]{2,1,0:T(8,128)(2,1)} %bitcast.7, s32[128,1024]{1,0:T(8,128)} %copy.12.perm_ref, f32[1,8192]{1,0:T(1,128)} %mul.64.w_ref), custom_call_target="tpu_custom_call" | custom-call | tf_op jit(solution)/shard_map/pallas_call | solution.py:188
  103.1 1.9 %copy.15 = f32[1,512,256]{2,1,0:T(8,128)} copy(f32[1,512,256]{2,1,0:T(8,128)} %bitcast.10) | data formatting | bytes 1048576
  (4 shorter events, 0.0 us)
Async XLA Ops:
  0.0 0.7 copy-start
